TPU v7x, 512 devices: a whole 4x4x16 slice. The times are simulated.
512 devices in a mesh: dp: 4 (over x), ctx: 16 (over z), tp: 8 (over y, core).
Axes of the slice: x: 4, y: 4, z: 16, core: 2. Of those that a mesh axis runs over, the one named last changes fastest.
Arguments:
- inputs: bfloat16 [4, 4096, 8192], P('dp', 'ctx', 'tp'), may hold values from -6 to 6
- cotangent: bfloat16 [4, 4096, 8192], P('dp', 'ctx', 'tp'), may hold values from -6 to 6
- residues: float32 [512, 16], P('tp'), may hold values from -3 to 3
- decay_rates: float32 [512, 16], P('tp'), may hold values from 4.8828125e-05 to 0.0333333333
- skip_gain: float32 [8192], P('tp'), may hold values from -1 to 1
Outputs:
- outputs: bfloat16 [4, 4096, 8192], P('dp', 'ctx', 'tp')
- grad_inputs: bfloat16 [4, 4096, 8192], P('dp', 'ctx', 'tp')
- grad_residues: float32 [512, 16], P('tp')
- grad_skip: float32 [8192], P('tp')
All inputs are finite; a program needn't handle non-finite values.
Results may differ from a plain program's by a relative error of at most 0.0014.
Values sent between devices are 32-bit elements; how exact they have to be, the bound alone decides.
A program may use at most 64 MiB of HBM per device.

v0:
```python
import math
import jax
import jax.numpy as jnp
from jax import lax
from jax.sharding import PartitionSpec as P

highest = lax.Precision.HIGHEST


def passed_along(value, axis, by):
    length = lax.axis_size(axis)
    pairs = [(i, i + by) for i in range(length) if 0 <= i + by < length]
    return lax.ppermute(value, axis, pairs)


def shards(inputs, cotangent, residues, decay_rates, skip_gain):
    local_batch, block_rows, channels = inputs.shape
    group_count, mode_count = residues.shape
    group_width = channels // group_count
    sub_rows = math.gcd(256, block_rows)
    sub_count = block_rows // sub_rows
    weight = jnp.sqrt(1.0 - jnp.exp(-2.0 * decay_rates))
    coefficient = residues * weight
    positions = jnp.arange(sub_rows, dtype=jnp.float32)
    center = (sub_rows - 1) / 2.0
    rate_cube = decay_rates[:, :, None]
    decay_down = jnp.exp(-rate_cube * (positions - center))
    decay_up = jnp.exp(rate_cube * (positions - center))
    from_start = jnp.exp(-rate_cube * positions)
    to_end = jnp.exp(-rate_cube * (sub_rows - 1.0 - positions))
    five_shape = (local_batch, sub_count, sub_rows, group_count, group_width)
    state_shape = (local_batch, mode_count, channels)
    state_split = (local_batch, mode_count, group_count, group_width)
    inputs_wide = inputs.astype(jnp.float32).reshape(five_shape)
    cotangent_wide = cotangent.astype(jnp.float32).reshape(five_shape)
    sub_ends = jnp.einsum("gmt,bktgc->kbmgc", to_end, inputs_wide, precision=highest)
    sub_starts = jnp.einsum("gmt,bktgc->kbmgc", from_start, cotangent_wide, precision=highest)
    device_end = sub_ends[0]
    device_start = sub_starts[sub_count - 1]
    end_states = device_end.reshape(state_shape)
    start_states = device_start.reshape(state_shape)
    channel_rates = jnp.repeat(decay_rates.T, group_width, axis=1) * float(block_rows)
    passing = jnp.exp(-channel_rates)

    def relay_turn(turn, carried):
        incoming_x, incoming_d = carried
        sent_x = incoming_x * passing + end_states
        sent_d = incoming_d * passing + start_states
        return (passed_along(sent_x, "ctx", 1), passed_along(sent_d, "ctx", -1))

    empty_states = jnp.zeros_like(end_states)
    state_before, state_after = lax.fori_loop(
        0, lax.axis_size("ctx") - 1, relay_turn, (empty_states, empty_states)
    )
    block_count = math.gcd(group_count, 16)
    per_block = group_count // block_count
    causal_mask = positions[:, None] >= positions[None, :]

    def by_groups(array):
        return array.reshape((block_count, per_block) + array.shape[1:])

    def data_blocks(array):
        return array.reshape(
            local_batch, sub_count, sub_rows, block_count, per_block, group_width
        ).transpose(3, 0, 1, 2, 4, 5)

    def local_block(pieces):
        coef_piece, down_piece, up_piece, weight_piece, wide_x, wide_d, half_x, half_d = pieces
        kernel = jnp.where(
            causal_mask,
            jnp.einsum("gm,gmt,gms->gts", coef_piece, down_piece, up_piece, precision=highest),
            0.0,
        )
        local_out = jnp.einsum("gts,bksgc->bktgc", kernel, wide_x, precision=highest)
        local_back = jnp.einsum("gts,bktgc->bksgc", kernel, wide_d, precision=highest)
        pairs = jnp.einsum("bktgc,bksgc->gts", half_d, half_x, preferred_element_type=jnp.float32)
        pairs = jnp.where(causal_mask, pairs, 0.0)
        local_grad = weight_piece * jnp.einsum(
            "gmt,gts,gms->gm", down_piece, pairs, up_piece, precision=highest
        )
        return (local_out, local_back, local_grad)

    half_inputs = inputs.reshape(five_shape)
    half_cotangent = cotangent.reshape(five_shape)
    block_out, block_back, block_grad = lax.map(
        local_block,
        (
            by_groups(coefficient),
            by_groups(decay_down),
            by_groups(decay_up),
            by_groups(weight),
            data_blocks(inputs_wide),
            data_blocks(cotangent_wide),
            data_blocks(half_inputs),
            data_blocks(half_cotangent),
        ),
    )
    local_out = block_out.transpose(1, 2, 3, 0, 4, 5).reshape(five_shape)
    local_back = block_back.transpose(1, 2, 3, 0, 4, 5).reshape(five_shape)
    local_grad = block_grad.reshape(group_count, mode_count)
    running = state_before.reshape(state_split)
    before_list = [running]
    running = state_after.reshape(state_split)
    after_list = [None] * sub_count
    after_list[0] = running
    before_stack = jnp.stack(before_list, axis=1)
    after_stack = jnp.stack(after_list, axis=1)
    first_weights = coefficient[:, :, None] * jnp.exp(-rate_cube * (positions + 1.0))
    last_weights = coefficient[:, :, None] * jnp.exp(-rate_cube * (sub_rows - positions))
    carried_out = jnp.einsum("gmt,bkmgc->bktgc", first_weights, before_stack, precision=highest)
    carried_back = jnp.einsum("gmt,bkmgc->bktgc", last_weights, after_stack, precision=highest)
    carried_grad = (
        weight
        * jnp.exp(-decay_rates)
        * jnp.einsum("kbmgc,bkmgc->gm", sub_starts, before_stack, precision=highest)
    )
    skip_wide = skip_gain.reshape(group_count, group_width)
    outputs = (
        (local_out + carried_out + skip_wide * inputs_wide)
        .reshape(local_batch, block_rows, channels)
        .astype(jnp.bfloat16)
    )
    grad_inputs = (
        (local_back + carried_back + skip_wide * cotangent_wide)
        .reshape(local_batch, block_rows, channels)
        .astype(jnp.bfloat16)
    )
    token_total = local_batch * block_rows * lax.axis_size("dp") * lax.axis_size("ctx")
    scale = 1.0 / math.sqrt(token_total)
    skip_local = jnp.sum(inputs_wide * cotangent_wide, axis=(0, 1, 2)).reshape(channels)
    grad_residues, grad_skip = lax.psum(
        ((local_grad + carried_grad) * scale, skip_local * scale), ("dp", "ctx")
    )
    return (outputs, grad_inputs, grad_residues, grad_skip)


def solution(mesh):
    placed = (P("dp", "ctx", "tp"), P("dp", "ctx", "tp"), P("tp", None), P("tp", None), P("tp"))
    return jax.shard_map(
        shards,
        mesh=mesh,
        in_specs=placed,
        out_specs=(P("dp", "ctx", "tp"), P("dp", "ctx", "tp"), P("tp", None), P("tp")),
        check_vma=False,
    )
```

profile of v0, /device:TPU:16, one launch (start us, length us, event | category | flops | bytes accessed | tf_op | source)
XLA Modules:
  0.0 629.1 jit_solution(2040821487755064121)
XLA Ops:
  6.7 172.4 %while.30 = (s32[]{:T(128)}, f32[16,1,1,256,4,16]{3,5,4,2,1,0:T(8,128)}, f32[16,1,1,256,4,16]{3,5,4,2,1,0:T(8,128)}, f32[16,4,16]{2,1,0:T(4,128)S(1)}, f32[16,1,...) while((s32[]{:T(128)}, ...), condition=%wide.region_1.0_spmd.clone.clone, body=%wide.region_0.0_spmd.clone.clone.sunk | while | flops 210354176 | bytes 6303369 | solution.py:85
  8.8 2.5 fusion.85
  14.7 2.7 fusion.87
  19.6 2.5 fusion.85
  25.4 2.7 fusion.87
  30.3 2.5 fusion.85
  36.2 2.7 fusion.87
  41.1 2.4 fusion.85
  47.0 2.7 fusion.87
  51.9 2.5 fusion.85
  57.7 2.7 fusion.87
  62.7 2.5 fusion.85
  68.5 2.7 fusion.87
  79.3 2.7 fusion.87
  84.2 2.5 fusion.85
  90.1 2.7 fusion.87
  95.0 2.4 fusion.85
  100.9 2.7 fusion.87
  111.7 2.7 fusion.87
  122.4 2.7 fusion.87
  127.3 2.4 fusion.85
  133.2 2.7 fusion.87
  138.1 2.4 fusion.85
  144.0 2.7 fusion.87
  148.9 2.5 fusion.85
  154.8 2.7 fusion.87
  159.7 2.4 fusion.85
  165.5 2.7 fusion.87
  170.4 2.5 fusion.85
  176.3 2.7 fusion.87
  184.8 158.3 %while.29 = (s32[]{:T(128)}, f32[1,16,1024]{2,1,0:T(8,128)S(1)}, f32[1,16,1024]{2,1,0:T(8,128)S(1)}, f32[1,16,1024]{2,1,0:T(8,128)S(1)}, f32[1,16,1024]{2,1,0:T(8,128)S(1)}, /*index=5*/f32[16,64]{1,0:T(8,128)S(1)}, s32[]{:T(128)}) while((s32[]{:T(128)}, f32[1,16,1024]{2,1,0:T(8,128)S(1)}, f32[1,16,1024]{2,1,0:T(8,128)S(1)}, ...), condition=%wide.region_3.4_spmd.clone, body=%wide.region_2.3_spmd.clone.sunk | while | flops 65538 | bytes 1183901 | solution.py:52
  185.3 3.8 collective-permute-start
  191.0 4.3 collective-permute-done.1
  195.8 3.8 collective-permute-start
  201.5 5.3 collective-permute-done.1
  207.3 5.1 collective-permute-start
  214.3 4.3 collective-permute-done.1
  219.1 3.9 collective-permute-start
  224.9 4.3 collective-permute-done.1
  229.7 4.8 collective-permute-start
  236.3 4.3 collective-permute-done.1
  241.1 5.1 collective-permute-start
  248.1 4.3 collective-permute-done.1
  252.9 3.9 collective-permute-start
  259.0 4.4 collective-permute-done.1
  263.9 3.9 collective-permute-start
  269.7 4.3 collective-permute-done.1
  274.5 2.8 collective-permute-start
  279.2 4.3 collective-permute-done.1
  284.0 3.3 collective-permute-start
  289.2 4.3 collective-permute-done.1
  293.9 3.1 collective-permute-start
  299.0 4.3 collective-permute-done.1
  303.7 3.3 collective-permute-start
  308.9 4.3 collective-permute-done.1
  313.7 3.4 collective-permute-start
  319.1 4.6 collective-permute-done.1
  324.2 3.4 collective-permute-start
  329.5 4.3 collective-permute-done.1
  334.2 2.7 collective-permute-start
  338.9 4.3 collective-permute-done.1
  343.9 3.3 fusion.34
  348.4 2.5 fusion.33
  353.2 275.2 %all-reduce = (f32[64,16]{1,0:T(8,128)S(1)}, f32[1024]{0:T(1024)}) all-reduce(f32[64,16]{1,0:T(8,128)S(1)} %add_multiply_fusion, f32[1024]{0:T(1024)S(1)} %broadcast_multiply_fusion), channel_id=1, replica_groups=mesh['dp'=4,'ctx'=16,'tp'=8] {'dp','ctx'}, use_global_device_ids=true, to_apply=%region_4.5 | all-reduce | flops 2048 | bytes 16384 | tf_op jit(solution)/shard_map/psum | solution.py:131
  (257 shorter events, 148.2 us)
Async XLA Ops:
  0.6 0.8 copy-start.6
  1.6 1.7 copy-start
  3.3 1.2 copy-start.1
  180.9 0.8 copy-start.3
  184.1 0.7 copy-start.5
  185.3 5.7 collective-permute-start
  189.1 6.2 collective-permute-start.1
  195.8 5.7 collective-permute-start
  199.6 7.2 %collective-permute-start.1 = (f32[1,16,1024]{2,1,0:T(8,128)S(1)}, f32[1,16,1024]{2,1,0:T(8,128)S(1)}, u32[]{:S(2)}, u32[]{:S(2)}) collective-permute-start(f32[1,16,1024]{2,1,0:T(8,128)S(1)} %get-tuple-element.351), channel_id=1, source_target_pairs={{8,0},{16,8},{24,16},{32,24},{40,32},{48,40},{56,48},{64,56},{72,6... | collective-permute-start | bytes 196616 | tf_op jit(solution)/shard_map/while/body/eval_jaxpr/ppermute | solution.py:13
  207.3 7.0 %collective-permute-start = (f32[1,16,1024]{2,1,0:T(8,128)S(1)}, f32[1,16,1024]{2,1,0:T(8,128)S(1)}, u32[]{:S(2)}, u32[]{:S(2)}) collective-permute-start(f32[1,16,1024]{2,1,0:T(8,128)S(1)} %get-tuple-element.350), channel_id=1, source_target_pairs={{0,8},{8,16},{16,24},{24,32},{32,40},{40,48},{48,56},{56,64},{64,7... | collective-permute-start | bytes 196616 | tf_op jit(solution)/shard_map/while/body/eval_jaxpr/ppermute | solution.py:13
  212.4 6.2 collective-permute-start.1
  219.1 5.8 collective-permute-start
  223.0 6.2 collective-permute-start.1
  229.7 6.6 %collective-permute-start = (f32[1,16,1024]{2,1,0:T(8,128)S(1)}, f32[1,16,1024]{2,1,0:T(8,128)S(1)}, u32[]{:S(2)}, u32[]{:S(2)}) collective-permute-start(f32[1,16,1024]{2,1,0:T(8,128)S(1)} %get-tuple-element.350), channel_id=1, source_target_pairs={{0,8},{8,16},{16,24},{24,32},{32,40},{40,48},{48,56},{56,64},{64,7... | collective-permute-start | bytes 196616 | tf_op jit(solution)/shard_map/while/body/eval_jaxpr/ppermute | solution.py:13
  234.4 6.2 collective-permute-start.1
  241.1 7.0 %collective-permute-start = (f32[1,16,1024]{2,1,0:T(8,128)S(1)}, f32[1,16,1024]{2,1,0:T(8,128)S(1)}, u32[]{:S(2)}, u32[]{:S(2)}) collective-permute-start(f32[1,16,1024]{2,1,0:T(8,128)S(1)} %get-tuple-element.350), channel_id=1, source_target_pairs={{0,8},{8,16},{16,24},{24,32},{32,40},{40,48},{48,56},{56,64},{64,7... | collective-permute-start | bytes 196616 | tf_op jit(solution)/shard_map/while/body/eval_jaxpr/ppermute | solution.py:13
  246.2 6.2 collective-permute-start.1
  252.9 6.1 collective-permute-start
  256.8 6.6 %collective-permute-start.1 = (f32[1,16,1024]{2,1,0:T(8,128)S(1)}, f32[1,16,1024]{2,1,0:T(8,128)S(1)}, u32[]{:S(2)}, u32[]{:S(2)}) collective-permute-start(f32[1,16,1024]{2,1,0:T(8,128)S(1)} %get-tuple-element.351), channel_id=1, source_target_pairs={{8,0},{16,8},{24,16},{32,24},{40,32},{48,40},{56,48},{64,56},{72,6... | collective-permute-start | bytes 196616 | tf_op jit(solution)/shard_map/while/body/eval_jaxpr/ppermute | solution.py:13
  263.9 5.8 collective-permute-start
  267.8 6.2 collective-permute-start.1
  274.5 4.7 collective-permute-start
  277.3 6.2 collective-permute-start.1
  284.0 5.2 collective-permute-start
  287.3 6.2 collective-permute-start.1
  293.9 5.0 collective-permute-start
  297.1 6.2 collective-permute-start.1
  303.7 5.2 collective-permute-start
  307.0 6.2 collective-permute-start.1
  313.7 5.4 collective-permute-start
  317.1 6.5 %collective-permute-start.1 = (f32[1,16,1024]{2,1,0:T(8,128)S(1)}, f32[1,16,1024]{2,1,0:T(8,128)S(1)}, u32[]{:S(2)}, u32[]{:S(2)}) collective-permute-start(f32[1,16,1024]{2,1,0:T(8,128)S(1)} %get-tuple-element.351), channel_id=1, source_target_pairs={{8,0},{16,8},{24,16},{32,24},{40,32},{48,40},{56,48},{64,56},{72,6... | collective-permute-start | bytes 196616 | tf_op jit(solution)/shard_map/while/body/eval_jaxpr/ppermute | solution.py:13
  324.2 5.3 collective-permute-start
  327.6 6.2 collective-permute-start.1
  334.2 4.6 collective-permute-start
  337.0 6.2 collective-permute-start.1
  343.1 0.7 copy-start.7
  350.9 1.0 copy-start.4
  352.0 1.0 copy-start.2
where the time goes:
time: 634 us; the launch traced here: 629 us
  blocking collectives  275 us (43%)
  matrix products  163 us (26%)
  starting transfers between devices  75.9 us (12%)
  waiting for transfers between devices  74.7 us (12%)
  local copies, waits for them, and re-layouts  34.5 us (5%)
    psum x1, blocking collectives, shards(): lax.psum(((local_grad + carried_grad) * scale, skip_local * scale), ('dp'...  275 us
    ppermute x30, starting transfers between devices, passed_along(): return lax.ppermute(value, axis, pairs)  75.9 us
    ppermute x30, waiting for transfers between devices, passed_along(): return lax.ppermute(value, axis, pairs)  74.7 us
    dot_general x16, matrix products, local_block(): jnp.einsum('gmt,gts,gms->gm', down_piece, pairs, up_piece, precision=high...  43.6 us
    dot_general x16, matrix products, local_block(): jnp.einsum('gts,bksgc->bktgc', kernel, wide_x, precision=highest)  39.2 us
    dot_general x16, matrix products, local_block(): jnp.einsum('gm,gmt,gms->gts', coef_piece, down_piece, up_piece, precision...  32.7 us
    dot_general x16, matrix products, local_block(): jnp.einsum('gts,bktgc->bksgc', kernel, wide_d, precision=highest)  19.9 us
    dot_general x16, matrix products, local_block(): jnp.einsum('bktgc,bksgc->gts', half_d, half_x, preferred_element_type=jnp...  17.8 us
  transfers between devices with their start and end apart: 30, of which 30 were waited for; matrix products, arithmetic and copies ran while one was open for 0% of the time, Pallas kernels for 0%

commit v1 on v0

--- a/solution.py
+++ b/solution.py
@@ -3,6 +3,7 @@
 import jax.numpy as jnp
 from jax import lax
 from jax.sharding import PartitionSpec as P
+from jax.lax import psum
 
 highest = lax.Precision.HIGHEST
 
@@ -128,8 +129,8 @@
     token_total = local_batch * block_rows * lax.axis_size("dp") * lax.axis_size("ctx")
     scale = 1.0 / math.sqrt(token_total)
     skip_local = jnp.sum(inputs_wide * cotangent_wide, axis=(0, 1, 2)).reshape(channels)
-    grad_residues, grad_skip = lax.psum(
-        ((local_grad + carried_grad) * scale, skip_local * scale), ("dp", "ctx")
+    grad_residues, grad_skip = psum(
+        psum(((local_grad + carried_grad) * scale, skip_local * scale), "ctx"), axis_name="dp"
     )
     return (outputs, grad_inputs, grad_residues, grad_skip)
 

time: 634 us -> 430 us (0.68)
  the two profiles are of different devices: /device:TPU:16 before, /device:TPU:8 now
where the time goes in v1:
time: 430 us; the launch traced here: 425 us
  matrix products  163 us (38%)
  starting transfers between devices  76 us (18%)
  waiting for transfers between devices  74.6 us (17%)
  blocking collectives  71.7 us (17%)
  local copies, waits for them, and re-layouts  33.9 us (8%)
    ppermute x30, starting transfers between devices, passed_along(): return lax.ppermute(value, axis, pairs)  76 us
    ppermute x30, waiting for transfers between devices, passed_along(): return lax.ppermute(value, axis, pairs)  74.6 us
    psum x1, blocking collectives, shards(): psum(((local_grad + carried_grad) * scale, skip_local * scale), 'ctx')  53.8 us
    dot_general x16, matrix products, local_block(): jnp.einsum('gmt,gts,gms->gm', down_piece, pairs, up_piece, precision=high...  43.6 us
    dot_general x16, matrix products, local_block(): jnp.einsum('gts,bksgc->bktgc', kernel, wide_x, precision=highest)  39.2 us
    dot_general x16, matrix products, local_block(): jnp.einsum('gm,gmt,gms->gts', coef_piece, down_piece, up_piece, precision...  32.7 us
    dot_general x16, matrix products, local_block(): jnp.einsum('gts,bktgc->bksgc', kernel, wide_d, precision=highest)  19.9 us
    psum x1, blocking collectives, shards(): psum(psum(((local_grad + carried_grad) * scale, skip_local * scale), 'ctx...  17.9 us
  transfers between devices with their start and end apart: 30, of which 30 were waited for; matrix products, arithmetic and copies ran while one was open for 0% of the time, Pallas kernels for 0%

profile of v1, /device:TPU:8, one launch (start us, length us, event | category | flops | bytes accessed | tf_op | source)
XLA Modules:
  0.0 425.0 jit_solution(14888512903051407676)
XLA Ops:
  6.7 172.4 %while.30 = (s32[]{:T(128)}, f32[16,1,1,256,4,16]{3,5,4,2,1,0:T(8,128)}, f32[16,1,1,256,4,16]{3,5,4,2,1,0:T(8,128)}, f32[16,4,16]{2,1,0:T(4,128)S(1)}, f32[16,1,...) while((s32[]{:T(128)}, ...), condition=%wide.region_1.0_spmd.clone.clone, body=%wide.region_0.0_spmd.clone.clone.sunk | while | flops 210354176 | bytes 6303369 | solution.py:86
  8.8 2.4 fusion.85
  14.7 2.7 fusion.87
  19.6 2.5 fusion.85
  25.5 2.7 fusion.87
  30.4 2.5 fusion.85
  36.2 2.7 fusion.87
  41.2 2.5 fusion.85
  47.0 2.7 fusion.87
  51.9 2.4 fusion.85
  57.8 2.7 fusion.87
  62.7 2.5 fusion.85
  68.6 2.7 fusion.87
  73.5 2.5 fusion.85
  79.4 2.7 fusion.87
  90.1 2.7 fusion.87
  95.0 2.5 fusion.85
  100.9 2.7 fusion.87
  105.8 2.4 fusion.85
  111.7 2.7 fusion.87
  122.5 2.7 fusion.87
  133.2 2.7 fusion.87
  138.2 2.4 fusion.85
  144.0 2.7 fusion.87
  148.9 2.4 fusion.85
  154.8 2.7 fusion.87
  159.7 2.5 fusion.85
  165.6 2.7 fusion.87
  176.4 2.7 fusion.87
  184.0 158.4 %while.29 = (s32[]{:T(128)}, f32[1,16,1024]{2,1,0:T(8,128)S(1)}, f32[1,16,1024]{2,1,0:T(8,128)S(1)}, f32[1,16,1024]{2,1,0:T(8,128)S(1)}, f32[1,16,1024]{2,1,0:T(8,128)S(1)}, /*index=5*/f32[16,64]{1,0:T(8,128)S(1)}, s32[]{:T(128)}) while((s32[]{:T(128)}, f32[1,16,1024]{2,1,0:T(8,128)S(1)}, f32[1,16,1024]{2,1,0:T(8,128)S(1)}, ...), condition=%wide.region_3.4_spmd.clone, body=%wide.region_2.3_spmd.clone.sunk | while | flops 65538 | bytes 1183901 | solution.py:53
  184.5 3.8 collective-permute-start
  190.2 4.3 %collective-permute-done.1 = f32[1,16,1024]{2,1,0:T(8,128)S(1)} collective-permute-done((f32[1,16,1024]{2,1,0:T(8,128)S(1)}, f32[1,16,1024]{2,1,0:T(8,128)S(1)}, u32[]{:S(2)}, u32[]{:S(2)}) %collective-permute-start.1) | collective-permute-done | bytes 65568 | tf_op jit(solution)/shard_map/while/body/eval_jaxpr/ppermute | solution.py:14
  195.0 3.8 collective-permute-start
  200.7 5.3 %collective-permute-done.1 = f32[1,16,1024]{2,1,0:T(8,128)S(1)} collective-permute-done((f32[1,16,1024]{2,1,0:T(8,128)S(1)}, f32[1,16,1024]{2,1,0:T(8,128)S(1)}, u32[]{:S(2)}, u32[]{:S(2)}) %collective-permute-start.1) | collective-permute-done | bytes 65568 | tf_op jit(solution)/shard_map/while/body/eval_jaxpr/ppermute | solution.py:14
  206.5 5.1 %collective-permute-start = (f32[1,16,1024]{2,1,0:T(8,128)S(1)}, f32[1,16,1024]{2,1,0:T(8,128)S(1)}, u32[]{:S(2)}, u32[]{:S(2)}) collective-permute-start(f32[1,16,1024]{2,1,0:T(8,128)S(1)} %get-tuple-element.352), channel_id=1, source_target_pairs={{0,8},{8,16},{16,24},{24,32},{32,40},{40,48},{48,56},{56,64},{64,7... | collective-permute-start | bytes 196616 | tf_op jit(solution)/shard_map/while/body/eval_jaxpr/ppermute | solution.py:14
  213.5 4.3 %collective-permute-done.1 = f32[1,16,1024]{2,1,0:T(8,128)S(1)} collective-permute-done((f32[1,16,1024]{2,1,0:T(8,128)S(1)}, f32[1,16,1024]{2,1,0:T(8,128)S(1)}, u32[]{:S(2)}, u32[]{:S(2)}) %collective-permute-start.1) | collective-permute-done | bytes 65568 | tf_op jit(solution)/shard_map/while/body/eval_jaxpr/ppermute | solution.py:14
  218.3 3.9 collective-permute-start
  224.1 4.3 %collective-permute-done.1 = f32[1,16,1024]{2,1,0:T(8,128)S(1)} collective-permute-done((f32[1,16,1024]{2,1,0:T(8,128)S(1)}, f32[1,16,1024]{2,1,0:T(8,128)S(1)}, u32[]{:S(2)}, u32[]{:S(2)}) %collective-permute-start.1) | collective-permute-done | bytes 65568 | tf_op jit(solution)/shard_map/while/body/eval_jaxpr/ppermute | solution.py:14
  228.9 4.8 %collective-permute-start = (f32[1,16,1024]{2,1,0:T(8,128)S(1)}, f32[1,16,1024]{2,1,0:T(8,128)S(1)}, u32[]{:S(2)}, u32[]{:S(2)}) collective-permute-start(f32[1,16,1024]{2,1,0:T(8,128)S(1)} %get-tuple-element.352), channel_id=1, source_target_pairs={{0,8},{8,16},{16,24},{24,32},{32,40},{40,48},{48,56},{56,64},{64,7... | collective-permute-start | bytes 196616 | tf_op jit(solution)/shard_map/while/body/eval_jaxpr/ppermute | solution.py:14
  235.6 4.3 %collective-permute-done.1 = f32[1,16,1024]{2,1,0:T(8,128)S(1)} collective-permute-done((f32[1,16,1024]{2,1,0:T(8,128)S(1)}, f32[1,16,1024]{2,1,0:T(8,128)S(1)}, u32[]{:S(2)}, u32[]{:S(2)}) %collective-permute-start.1) | collective-permute-done | bytes 65568 | tf_op jit(solution)/shard_map/while/body/eval_jaxpr/ppermute | solution.py:14
  240.3 5.1 %collective-permute-start = (f32[1,16,1024]{2,1,0:T(8,128)S(1)}, f32[1,16,1024]{2,1,0:T(8,128)S(1)}, u32[]{:S(2)}, u32[]{:S(2)}) collective-permute-start(f32[1,16,1024]{2,1,0:T(8,128)S(1)} %get-tuple-element.352), channel_id=1, source_target_pairs={{0,8},{8,16},{16,24},{24,32},{32,40},{40,48},{48,56},{56,64},{64,7... | collective-permute-start | bytes 196616 | tf_op jit(solution)/shard_map/while/body/eval_jaxpr/ppermute | solution.py:14
  247.4 4.3 %collective-permute-done.1 = f32[1,16,1024]{2,1,0:T(8,128)S(1)} collective-permute-done((f32[1,16,1024]{2,1,0:T(8,128)S(1)}, f32[1,16,1024]{2,1,0:T(8,128)S(1)}, u32[]{:S(2)}, u32[]{:S(2)}) %collective-permute-start.1) | collective-permute-done | bytes 65568 | tf_op jit(solution)/shard_map/while/body/eval_jaxpr/ppermute | solution.py:14
  252.1 3.9 collective-permute-start
  258.3 4.3 %collective-permute-done.1 = f32[1,16,1024]{2,1,0:T(8,128)S(1)} collective-permute-done((f32[1,16,1024]{2,1,0:T(8,128)S(1)}, f32[1,16,1024]{2,1,0:T(8,128)S(1)}, u32[]{:S(2)}, u32[]{:S(2)}) %collective-permute-start.1) | collective-permute-done | bytes 65568 | tf_op jit(solution)/shard_map/while/body/eval_jaxpr/ppermute | solution.py:14
  263.1 3.9 collective-permute-start
  268.9 4.3 %collective-permute-done.1 = f32[1,16,1024]{2,1,0:T(8,128)S(1)} collective-permute-done((f32[1,16,1024]{2,1,0:T(8,128)S(1)}, f32[1,16,1024]{2,1,0:T(8,128)S(1)}, u32[]{:S(2)}, u32[]{:S(2)}) %collective-permute-start.1) | collective-permute-done | bytes 65568 | tf_op jit(solution)/shard_map/while/body/eval_jaxpr/ppermute | solution.py:14
  273.7 2.8 collective-permute-start
  278.4 4.3 %collective-permute-done.1 = f32[1,16,1024]{2,1,0:T(8,128)S(1)} collective-permute-done((f32[1,16,1024]{2,1,0:T(8,128)S(1)}, f32[1,16,1024]{2,1,0:T(8,128)S(1)}, u32[]{:S(2)}, u32[]{:S(2)}) %collective-permute-start.1) | collective-permute-done | bytes 65568 | tf_op jit(solution)/shard_map/while/body/eval_jaxpr/ppermute | solution.py:14
  283.2 3.3 collective-permute-start
  288.4 4.3 %collective-permute-done.1 = f32[1,16,1024]{2,1,0:T(8,128)S(1)} collective-permute-done((f32[1,16,1024]{2,1,0:T(8,128)S(1)}, f32[1,16,1024]{2,1,0:T(8,128)S(1)}, u32[]{:S(2)}, u32[]{:S(2)}) %collective-permute-start.1) | collective-permute-done | bytes 65568 | tf_op jit(solution)/shard_map/while/body/eval_jaxpr/ppermute | solution.py:14
  293.1 3.1 collective-permute-start
  298.2 4.3 %collective-permute-done.1 = f32[1,16,1024]{2,1,0:T(8,128)S(1)} collective-permute-done((f32[1,16,1024]{2,1,0:T(8,128)S(1)}, f32[1,16,1024]{2,1,0:T(8,128)S(1)}, u32[]{:S(2)}, u32[]{:S(2)}) %collective-permute-start.1) | collective-permute-done | bytes 65568 | tf_op jit(solution)/shard_map/while/body/eval_jaxpr/ppermute | solution.py:14
  302.9 3.3 collective-permute-start
  308.2 4.3 %collective-permute-done.1 = f32[1,16,1024]{2,1,0:T(8,128)S(1)} collective-permute-done((f32[1,16,1024]{2,1,0:T(8,128)S(1)}, f32[1,16,1024]{2,1,0:T(8,128)S(1)}, u32[]{:S(2)}, u32[]{:S(2)}) %collective-permute-start.1) | collective-permute-done | bytes 65568 | tf_op jit(solution)/shard_map/while/body/eval_jaxpr/ppermute | solution.py:14
  312.9 3.4 collective-permute-start
  318.3 4.6 %collective-permute-done.1 = f32[1,16,1024]{2,1,0:T(8,128)S(1)} collective-permute-done((f32[1,16,1024]{2,1,0:T(8,128)S(1)}, f32[1,16,1024]{2,1,0:T(8,128)S(1)}, u32[]{:S(2)}, u32[]{:S(2)}) %collective-permute-start.1) | collective-permute-done | bytes 65568 | tf_op jit(solution)/shard_map/while/body/eval_jaxpr/ppermute | solution.py:14
  323.4 3.4 collective-permute-start
  328.7 4.3 %collective-permute-done.1 = f32[1,16,1024]{2,1,0:T(8,128)S(1)} collective-permute-done((f32[1,16,1024]{2,1,0:T(8,128)S(1)}, f32[1,16,1024]{2,1,0:T(8,128)S(1)}, u32[]{:S(2)}, u32[]{:S(2)}) %collective-permute-start.1) | collective-permute-done | bytes 65568 | tf_op jit(solution)/shard_map/while/body/eval_jaxpr/ppermute | solution.py:14
  333.5 2.8 collective-permute-start
  338.1 4.3 %collective-permute-done.1 = f32[1,16,1024]{2,1,0:T(8,128)S(1)} collective-permute-done((f32[1,16,1024]{2,1,0:T(8,128)S(1)}, f32[1,16,1024]{2,1,0:T(8,128)S(1)}, u32[]{:S(2)}, u32[]{:S(2)}) %collective-permute-start.1) | collective-permute-done | bytes 65568 | tf_op jit(solution)/shard_map/while/body/eval_jaxpr/ppermute | solution.py:14
  343.9 53.8 %all-reduce = (f32[64,16]{1,0:T(8,128)S(1)}, f32[1024]{0:T(1024)S(1)}) all-reduce(f32[64,16]{1,0:T(8,128)S(1)} %add_multiply_fusion, f32[1024]{0:T(1024)S(1)} %broadcast_multiply_fusion), channel_id=1, replica_groups=mesh['dp'=4,'ctx'=16,'tp'=8] {'ctx'}, use_global_device_ids=true, to_apply=%region_4.5 | all-reduce | flops 2048 | bytes 16384 | tf_op jit(solution)/shard_map/psum | solution.py:133
  397.7 17.9 %all-reduce.1 = (f32[64,16]{1,0:T(8,128)S(1)}, f32[1024]{0:T(1024)}) all-reduce(f32[64,16]{1,0:T(8,128)S(1)} %get-tuple-element.241, f32[1024]{0:T(1024)S(1)} %get-tuple-element.242), channel_id=1, replica_groups=mesh['dp'=4,'ctx'=16,'tp'=8] {'dp'}, use_global_device_ids=true, to_apply=%region_5.6 | all-reduce | flops 2048 | bytes 16384 | tf_op jit(solution)/shard_map/psum | solution.py:132
  417.0 3.3 fusion.34
  421.5 2.5 fusion.33
  (254 shorter events, 150.1 us)
Async XLA Ops:
  0.6 0.8 copy-start.4
  1.6 1.7 copy-start
  3.3 1.2 copy-start.1
  183.3 0.7 copy-start.3
  184.5 5.7 %collective-permute-start = (f32[1,16,1024]{2,1,0:T(8,128)S(1)}, f32[1,16,1024]{2,1,0:T(8,128)S(1)}, u32[]{:S(2)}, u32[]{:S(2)}) collective-permute-start(f32[1,16,1024]{2,1,0:T(8,128)S(1)} %get-tuple-element.352), channel_id=1, source_target_pairs={{0,8},{8,16},{16,24},{24,32},{32,40},{40,48},{48,56},{56,64},{64,7... | collective-permute-start | bytes 196616 | tf_op jit(solution)/shard_map/while/body/eval_jaxpr/ppermute | solution.py:14
  188.4 6.2 %collective-permute-start.1 = (f32[1,16,1024]{2,1,0:T(8,128)S(1)}, f32[1,16,1024]{2,1,0:T(8,128)S(1)}, u32[]{:S(2)}, u32[]{:S(2)}) collective-permute-start(f32[1,16,1024]{2,1,0:T(8,128)S(1)} %get-tuple-element.353), channel_id=1, source_target_pairs={{8,0},{16,8},{24,16},{32,24},{40,32},{48,40},{56,48},{64,56},{72,6... | collective-permute-start | bytes 196616 | tf_op jit(solution)/shard_map/while/body/eval_jaxpr/ppermute | solution.py:14
  195.0 5.7 %collective-permute-start = (f32[1,16,1024]{2,1,0:T(8,128)S(1)}, f32[1,16,1024]{2,1,0:T(8,128)S(1)}, u32[]{:S(2)}, u32[]{:S(2)}) collective-permute-start(f32[1,16,1024]{2,1,0:T(8,128)S(1)} %get-tuple-element.352), channel_id=1, source_target_pairs={{0,8},{8,16},{16,24},{24,32},{32,40},{40,48},{48,56},{56,64},{64,7... | collective-permute-start | bytes 196616 | tf_op jit(solution)/shard_map/while/body/eval_jaxpr/ppermute | solution.py:14
  198.9 7.2 %collective-permute-start.1 = (f32[1,16,1024]{2,1,0:T(8,128)S(1)}, f32[1,16,1024]{2,1,0:T(8,128)S(1)}, u32[]{:S(2)}, u32[]{:S(2)}) collective-permute-start(f32[1,16,1024]{2,1,0:T(8,128)S(1)} %get-tuple-element.353), channel_id=1, source_target_pairs={{8,0},{16,8},{24,16},{32,24},{40,32},{48,40},{56,48},{64,56},{72,6... | collective-permute-start | bytes 196616 | tf_op jit(solution)/shard_map/while/body/eval_jaxpr/ppermute | solution.py:14
  206.5 7.0 %collective-permute-start = (f32[1,16,1024]{2,1,0:T(8,128)S(1)}, f32[1,16,1024]{2,1,0:T(8,128)S(1)}, u32[]{:S(2)}, u32[]{:S(2)}) collective-permute-start(f32[1,16,1024]{2,1,0:T(8,128)S(1)} %get-tuple-element.352), channel_id=1, source_target_pairs={{0,8},{8,16},{16,24},{24,32},{32,40},{40,48},{48,56},{56,64},{64,7... | collective-permute-start | bytes 196616 | tf_op jit(solution)/shard_map/while/body/eval_jaxpr/ppermute | solution.py:14
  211.7 6.2 %collective-permute-start.1 = (f32[1,16,1024]{2,1,0:T(8,128)S(1)}, f32[1,16,1024]{2,1,0:T(8,128)S(1)}, u32[]{:S(2)}, u32[]{:S(2)}) collective-permute-start(f32[1,16,1024]{2,1,0:T(8,128)S(1)} %get-tuple-element.353), channel_id=1, source_target_pairs={{8,0},{16,8},{24,16},{32,24},{40,32},{48,40},{56,48},{64,56},{72,6... | collective-permute-start | bytes 196616 | tf_op jit(solution)/shard_map/while/body/eval_jaxpr/ppermute | solution.py:14
  218.3 5.8 %collective-permute-start = (f32[1,16,1024]{2,1,0:T(8,128)S(1)}, f32[1,16,1024]{2,1,0:T(8,128)S(1)}, u32[]{:S(2)}, u32[]{:S(2)}) collective-permute-start(f32[1,16,1024]{2,1,0:T(8,128)S(1)} %get-tuple-element.352), channel_id=1, source_target_pairs={{0,8},{8,16},{16,24},{24,32},{32,40},{40,48},{48,56},{56,64},{64,7... | collective-permute-start | bytes 196616 | tf_op jit(solution)/shard_map/while/body/eval_jaxpr/ppermute | solution.py:14
  222.2 6.2 %collective-permute-start.1 = (f32[1,16,1024]{2,1,0:T(8,128)S(1)}, f32[1,16,1024]{2,1,0:T(8,128)S(1)}, u32[]{:S(2)}, u32[]{:S(2)}) collective-permute-start(f32[1,16,1024]{2,1,0:T(8,128)S(1)} %get-tuple-element.353), channel_id=1, source_target_pairs={{8,0},{16,8},{24,16},{32,24},{40,32},{48,40},{56,48},{64,56},{72,6... | collective-permute-start | bytes 196616 | tf_op jit(solution)/shard_map/while/body/eval_jaxpr/ppermute | solution.py:14
  228.9 6.7 %collective-permute-start = (f32[1,16,1024]{2,1,0:T(8,128)S(1)}, f32[1,16,1024]{2,1,0:T(8,128)S(1)}, u32[]{:S(2)}, u32[]{:S(2)}) collective-permute-start(f32[1,16,1024]{2,1,0:T(8,128)S(1)} %get-tuple-element.352), channel_id=1, source_target_pairs={{0,8},{8,16},{16,24},{24,32},{32,40},{40,48},{48,56},{56,64},{64,7... | collective-permute-start | bytes 196616 | tf_op jit(solution)/shard_map/while/body/eval_jaxpr/ppermute | solution.py:14
  233.7 6.2 %collective-permute-start.1 = (f32[1,16,1024]{2,1,0:T(8,128)S(1)}, f32[1,16,1024]{2,1,0:T(8,128)S(1)}, u32[]{:S(2)}, u32[]{:S(2)}) collective-permute-start(f32[1,16,1024]{2,1,0:T(8,128)S(1)} %get-tuple-element.353), channel_id=1, source_target_pairs={{8,0},{16,8},{24,16},{32,24},{40,32},{48,40},{56,48},{64,56},{72,6... | collective-permute-start | bytes 196616 | tf_op jit(solution)/shard_map/while/body/eval_jaxpr/ppermute | solution.py:14
  240.3 7.0 %collective-permute-start = (f32[1,16,1024]{2,1,0:T(8,128)S(1)}, f32[1,16,1024]{2,1,0:T(8,128)S(1)}, u32[]{:S(2)}, u32[]{:S(2)}) collective-permute-start(f32[1,16,1024]{2,1,0:T(8,128)S(1)} %get-tuple-element.352), channel_id=1, source_target_pairs={{0,8},{8,16},{16,24},{24,32},{32,40},{40,48},{48,56},{56,64},{64,7... | collective-permute-start | bytes 196616 | tf_op jit(solution)/shard_map/while/body/eval_jaxpr/ppermute | solution.py:14
  245.5 6.2 %collective-permute-start.1 = (f32[1,16,1024]{2,1,0:T(8,128)S(1)}, f32[1,16,1024]{2,1,0:T(8,128)S(1)}, u32[]{:S(2)}, u32[]{:S(2)}) collective-permute-start(f32[1,16,1024]{2,1,0:T(8,128)S(1)} %get-tuple-element.353), channel_id=1, source_target_pairs={{8,0},{16,8},{24,16},{32,24},{40,32},{48,40},{56,48},{64,56},{72,6... | collective-permute-start | bytes 196616 | tf_op jit(solution)/shard_map/while/body/eval_jaxpr/ppermute | solution.py:14
  252.1 6.1 %collective-permute-start = (f32[1,16,1024]{2,1,0:T(8,128)S(1)}, f32[1,16,1024]{2,1,0:T(8,128)S(1)}, u32[]{:S(2)}, u32[]{:S(2)}) collective-permute-start(f32[1,16,1024]{2,1,0:T(8,128)S(1)} %get-tuple-element.352), channel_id=1, source_target_pairs={{0,8},{8,16},{16,24},{24,32},{32,40},{40,48},{48,56},{56,64},{64,7... | collective-permute-start | bytes 196616 | tf_op jit(solution)/shard_map/while/body/eval_jaxpr/ppermute | solution.py:14
  256.1 6.6 %collective-permute-start.1 = (f32[1,16,1024]{2,1,0:T(8,128)S(1)}, f32[1,16,1024]{2,1,0:T(8,128)S(1)}, u32[]{:S(2)}, u32[]{:S(2)}) collective-permute-start(f32[1,16,1024]{2,1,0:T(8,128)S(1)} %get-tuple-element.353), channel_id=1, source_target_pairs={{8,0},{16,8},{24,16},{32,24},{40,32},{48,40},{56,48},{64,56},{72,6... | collective-permute-start | bytes 196616 | tf_op jit(solution)/shard_map/while/body/eval_jaxpr/ppermute | solution.py:14
  263.1 5.8 %collective-permute-start = (f32[1,16,1024]{2,1,0:T(8,128)S(1)}, f32[1,16,1024]{2,1,0:T(8,128)S(1)}, u32[]{:S(2)}, u32[]{:S(2)}) collective-permute-start(f32[1,16,1024]{2,1,0:T(8,128)S(1)} %get-tuple-element.352), channel_id=1, source_target_pairs={{0,8},{8,16},{16,24},{24,32},{32,40},{40,48},{48,56},{56,64},{64,7... | collective-permute-start | bytes 196616 | tf_op jit(solution)/shard_map/while/body/eval_jaxpr/ppermute | solution.py:14
  267.0 6.2 %collective-permute-start.1 = (f32[1,16,1024]{2,1,0:T(8,128)S(1)}, f32[1,16,1024]{2,1,0:T(8,128)S(1)}, u32[]{:S(2)}, u32[]{:S(2)}) collective-permute-start(f32[1,16,1024]{2,1,0:T(8,128)S(1)} %get-tuple-element.353), channel_id=1, source_target_pairs={{8,0},{16,8},{24,16},{32,24},{40,32},{48,40},{56,48},{64,56},{72,6... | collective-permute-start | bytes 196616 | tf_op jit(solution)/shard_map/while/body/eval_jaxpr/ppermute | solution.py:14
  273.7 4.7 %collective-permute-start = (f32[1,16,1024]{2,1,0:T(8,128)S(1)}, f32[1,16,1024]{2,1,0:T(8,128)S(1)}, u32[]{:S(2)}, u32[]{:S(2)}) collective-permute-start(f32[1,16,1024]{2,1,0:T(8,128)S(1)} %get-tuple-element.352), channel_id=1, source_target_pairs={{0,8},{8,16},{16,24},{24,32},{32,40},{40,48},{48,56},{56,64},{64,7... | collective-permute-start | bytes 196616 | tf_op jit(solution)/shard_map/while/body/eval_jaxpr/ppermute | solution.py:14
  276.5 6.2 %collective-permute-start.1 = (f32[1,16,1024]{2,1,0:T(8,128)S(1)}, f32[1,16,1024]{2,1,0:T(8,128)S(1)}, u32[]{:S(2)}, u32[]{:S(2)}) collective-permute-start(f32[1,16,1024]{2,1,0:T(8,128)S(1)} %get-tuple-element.353), channel_id=1, source_target_pairs={{8,0},{16,8},{24,16},{32,24},{40,32},{48,40},{56,48},{64,56},{72,6... | collective-permute-start | bytes 196616 | tf_op jit(solution)/shard_map/while/body/eval_jaxpr/ppermute | solution.py:14
  283.2 5.2 %collective-permute-start = (f32[1,16,1024]{2,1,0:T(8,128)S(1)}, f32[1,16,1024]{2,1,0:T(8,128)S(1)}, u32[]{:S(2)}, u32[]{:S(2)}) collective-permute-start(f32[1,16,1024]{2,1,0:T(8,128)S(1)} %get-tuple-element.352), channel_id=1, source_target_pairs={{0,8},{8,16},{16,24},{24,32},{32,40},{40,48},{48,56},{56,64},{64,7... | collective-permute-start | bytes 196616 | tf_op jit(solution)/shard_map/while/body/eval_jaxpr/ppermute | solution.py:14
  286.5 6.2 %collective-permute-start.1 = (f32[1,16,1024]{2,1,0:T(8,128)S(1)}, f32[1,16,1024]{2,1,0:T(8,128)S(1)}, u32[]{:S(2)}, u32[]{:S(2)}) collective-permute-start(f32[1,16,1024]{2,1,0:T(8,128)S(1)} %get-tuple-element.353), channel_id=1, source_target_pairs={{8,0},{16,8},{24,16},{32,24},{40,32},{48,40},{56,48},{64,56},{72,6... | collective-permute-start | bytes 196616 | tf_op jit(solution)/shard_map/while/body/eval_jaxpr/ppermute | solution.py:14
  293.1 5.0 %collective-permute-start = (f32[1,16,1024]{2,1,0:T(8,128)S(1)}, f32[1,16,1024]{2,1,0:T(8,128)S(1)}, u32[]{:S(2)}, u32[]{:S(2)}) collective-permute-start(f32[1,16,1024]{2,1,0:T(8,128)S(1)} %get-tuple-element.352), channel_id=1, source_target_pairs={{0,8},{8,16},{16,24},{24,32},{32,40},{40,48},{48,56},{56,64},{64,7... | collective-permute-start | bytes 196616 | tf_op jit(solution)/shard_map/while/body/eval_jaxpr/ppermute | solution.py:14
  296.3 6.2 %collective-permute-start.1 = (f32[1,16,1024]{2,1,0:T(8,128)S(1)}, f32[1,16,1024]{2,1,0:T(8,128)S(1)}, u32[]{:S(2)}, u32[]{:S(2)}) collective-permute-start(f32[1,16,1024]{2,1,0:T(8,128)S(1)} %get-tuple-element.353), channel_id=1, source_target_pairs={{8,0},{16,8},{24,16},{32,24},{40,32},{48,40},{56,48},{64,56},{72,6... | collective-permute-start | bytes 196616 | tf_op jit(solution)/shard_map/while/body/eval_jaxpr/ppermute | solution.py:14
  302.9 5.2 %collective-permute-start = (f32[1,16,1024]{2,1,0:T(8,128)S(1)}, f32[1,16,1024]{2,1,0:T(8,128)S(1)}, u32[]{:S(2)}, u32[]{:S(2)}) collective-permute-start(f32[1,16,1024]{2,1,0:T(8,128)S(1)} %get-tuple-element.352), channel_id=1, source_target_pairs={{0,8},{8,16},{16,24},{24,32},{32,40},{40,48},{48,56},{56,64},{64,7... | collective-permute-start | bytes 196616 | tf_op jit(solution)/shard_map/while/body/eval_jaxpr/ppermute | solution.py:14
  306.3 6.2 %collective-permute-start.1 = (f32[1,16,1024]{2,1,0:T(8,128)S(1)}, f32[1,16,1024]{2,1,0:T(8,128)S(1)}, u32[]{:S(2)}, u32[]{:S(2)}) collective-permute-start(f32[1,16,1024]{2,1,0:T(8,128)S(1)} %get-tuple-element.353), channel_id=1, source_target_pairs={{8,0},{16,8},{24,16},{32,24},{40,32},{48,40},{56,48},{64,56},{72,6... | collective-permute-start | bytes 196616 | tf_op jit(solution)/shard_map/while/body/eval_jaxpr/ppermute | solution.py:14
  312.9 5.3 %collective-permute-start = (f32[1,16,1024]{2,1,0:T(8,128)S(1)}, f32[1,16,1024]{2,1,0:T(8,128)S(1)}, u32[]{:S(2)}, u32[]{:S(2)}) collective-permute-start(f32[1,16,1024]{2,1,0:T(8,128)S(1)} %get-tuple-element.352), channel_id=1, source_target_pairs={{0,8},{8,16},{16,24},{24,32},{32,40},{40,48},{48,56},{56,64},{64,7... | collective-permute-start | bytes 196616 | tf_op jit(solution)/shard_map/while/body/eval_jaxpr/ppermute | solution.py:14
  316.4 6.5 %collective-permute-start.1 = (f32[1,16,1024]{2,1,0:T(8,128)S(1)}, f32[1,16,1024]{2,1,0:T(8,128)S(1)}, u32[]{:S(2)}, u32[]{:S(2)}) collective-permute-start(f32[1,16,1024]{2,1,0:T(8,128)S(1)} %get-tuple-element.353), channel_id=1, source_target_pairs={{8,0},{16,8},{24,16},{32,24},{40,32},{48,40},{56,48},{64,56},{72,6... | collective-permute-start | bytes 196616 | tf_op jit(solution)/shard_map/while/body/eval_jaxpr/ppermute | solution.py:14
  323.4 5.3 %collective-permute-start = (f32[1,16,1024]{2,1,0:T(8,128)S(1)}, f32[1,16,1024]{2,1,0:T(8,128)S(1)}, u32[]{:S(2)}, u32[]{:S(2)}) collective-permute-start(f32[1,16,1024]{2,1,0:T(8,128)S(1)} %get-tuple-element.352), channel_id=1, source_target_pairs={{0,8},{8,16},{16,24},{24,32},{32,40},{40,48},{48,56},{56,64},{64,7... | collective-permute-start | bytes 196616 | tf_op jit(solution)/shard_map/while/body/eval_jaxpr/ppermute | solution.py:14
  326.8 6.2 %collective-permute-start.1 = (f32[1,16,1024]{2,1,0:T(8,128)S(1)}, f32[1,16,1024]{2,1,0:T(8,128)S(1)}, u32[]{:S(2)}, u32[]{:S(2)}) collective-permute-start(f32[1,16,1024]{2,1,0:T(8,128)S(1)} %get-tuple-element.353), channel_id=1, source_target_pairs={{8,0},{16,8},{24,16},{32,24},{40,32},{48,40},{56,48},{64,56},{72,6... | collective-permute-start | bytes 196616 | tf_op jit(solution)/shard_map/while/body/eval_jaxpr/ppermute | solution.py:14
  333.5 4.7 %collective-permute-start = (f32[1,16,1024]{2,1,0:T(8,128)S(1)}, f32[1,16,1024]{2,1,0:T(8,128)S(1)}, u32[]{:S(2)}, u32[]{:S(2)}) collective-permute-start(f32[1,16,1024]{2,1,0:T(8,128)S(1)} %get-tuple-element.352), channel_id=1, source_target_pairs={{0,8},{8,16},{16,24},{24,32},{32,40},{40,48},{48,56},{56,64},{64,7... | collective-permute-start | bytes 196616 | tf_op jit(solution)/shard_map/while/body/eval_jaxpr/ppermute | solution.py:14
  336.2 6.2 %collective-permute-start.1 = (f32[1,16,1024]{2,1,0:T(8,128)S(1)}, f32[1,16,1024]{2,1,0:T(8,128)S(1)}, u32[]{:S(2)}, u32[]{:S(2)}) collective-permute-start(f32[1,16,1024]{2,1,0:T(8,128)S(1)} %get-tuple-element.353), channel_id=1, source_target_pairs={{8,0},{16,8},{24,16},{32,24},{40,32},{48,40},{56,48},{64,56},{72,6... | collective-permute-start | bytes 196616 | tf_op jit(solution)/shard_map/while/body/eval_jaxpr/ppermute | solution.py:14
  342.6 1.0 copy-start.2
  416.2 0.7 copy-start.5
